TPU v7x, 32 devices: a whole 2x2x4 slice. The times are simulated.
32 devices in a mesh: seq: 8 (over z, x), head: 4 (over y, core).
Axes of the slice: x: 2, y: 2, z: 4, core: 2. Of those that a mesh axis runs over, the one named last changes fastest.
Arguments:
- query_heads: bfloat16 [4, 4, 64, 192], P(None, None, 'head'), may hold values from -6 to 6
- up_keys: bfloat16 [64, 128, 512], P('head'), may hold values from -0.5 to 0.5
- up_values: bfloat16 [64, 512, 128], P('head'), may hold values from -0.25 to 0.25
- latent_cache: bfloat16 [4, 65536, 576], P(None, ('seq', 'head')), may hold values from -120 to 120
- new_latent: bfloat16 [4, 4, 576], replicated, may hold values from -24 to 24
- context_lengths: int32 [4], replicated, may hold values from 8192 to 65536, as said below
- positions: int32 [4], replicated, may hold values from 0 to 65535
Outputs:
- attended: bfloat16 [4, 4, 64, 128], P(None, None, 'head')
Inputs may be any that keep to these rules, and one draw needn't show every extreme that they name: `context_lengths`: some request uses all 65536 cached positions.
All inputs are finite; a program needn't handle non-finite values.
Results may differ from a plain program's by a relative error of at most 0.019.
The roundings to bfloat16 on the way count: a program that leaves them out, or rounds other values in their place, can miss the bound.
Values may be sent and summed in bfloat16 or wider, within the bound.
A program may use at most 512 MiB of HBM per device.

v0:
```python
import jax
import jax.numpy as jnp
from jax import lax
from jax.sharding import PartitionSpec as P

rope_base = 50000.0
masked_score = -1e30


def rotate(values, where_at):
    halfway = values.shape[-1] // 2
    counter = jnp.arange(halfway, dtype=jnp.float32)
    inverse = jnp.power(jnp.float32(rope_base), -2.0 * counter / values.shape[-1])
    angles = where_at.astype(jnp.float32)[..., None] * inverse
    cosine = jnp.cos(angles)
    sine_part = jnp.sin(angles)
    leading = values[..., :halfway]
    trailing = values[..., halfway:]
    return jnp.concatenate(
        [leading * cosine - trailing * sine_part, trailing * cosine + leading * sine_part], axis=-1
    )


def build_new_keys(new_latent, pos_grid, latent_width):
    rotated = rotate(new_latent[..., latent_width:].astype(jnp.float32), pos_grid).astype(
        jnp.bfloat16
    )
    return jnp.concatenate([new_latent[..., :latent_width], rotated], axis=-1)


def own_heads(values, heads_own):
    start_head = lax.axis_index("head") * heads_own
    return lax.dynamic_slice_in_dim(values, start_head, heads_own, axis=2)


def project_values(latents, values_float):
    return jnp.einsum("bshc,hcv->bshv", latents, values_float, precision=lax.Precision.HIGHEST)


def on_device(
    query_heads, up_keys, up_values, latent_cache, new_latent, context_lengths, positions
):
    step_count, requests, heads_own, query_width = query_heads.shape
    nope_width = up_keys.shape[1]
    latent_width = up_keys.shape[2]
    cache_rows = latent_cache.shape[1]
    softmax_scale = float(query_width) ** (-0.5)
    values_float = up_values.astype(jnp.float32)
    pos_grid = positions[None, :] + jnp.arange(step_count, dtype=jnp.int32)[:, None]
    query_latent = jnp.einsum(
        "sbhn,hnc->sbhc", query_heads[..., :nope_width], up_keys, preferred_element_type=jnp.float32
    ).astype(jnp.bfloat16)
    query_rope = rotate(
        query_heads[..., nope_width:].astype(jnp.float32), pos_grid[:, :, None]
    ).astype(jnp.bfloat16)
    own_queries = jnp.concatenate([query_latent, query_rope], axis=-1)
    new_keys = build_new_keys(new_latent, pos_grid, latent_width)
    all_queries = lax.all_gather(own_queries, "head", axis=2, tiled=True)
    head_count = all_queries.shape[2]
    device_slot = lax.axis_index("seq") * lax.axis_size("head") + lax.axis_index("head")
    row_numbers = device_slot * cache_rows + jnp.arange(cache_rows, dtype=jnp.int32)

    def local_part(request_item):
        queries, cache_keys, length = request_item
        query_rows = queries.reshape(step_count * head_count, queries.shape[-1])
        scores = (
            jnp.einsum("qc,kc->qk", query_rows, cache_keys, preferred_element_type=jnp.float32)
            * softmax_scale
        )
        visible = (row_numbers < length)[None, :]
        scores = jnp.where(visible, scores, masked_score)
        highest = jnp.max(scores, axis=1)
        weights = jnp.where(visible, jnp.exp(scores - highest[:, None]), 0.0)
        weight_sum = jnp.sum(weights, axis=1)
        weighted = jnp.dot(
            weights.astype(jnp.bfloat16),
            cache_keys[:, :latent_width],
            preferred_element_type=jnp.float32,
        )
        return (highest, weight_sum, weighted)

    highest, weight_sum, weighted = lax.map(
        local_part, (jnp.swapaxes(all_queries, 0, 1), latent_cache, context_lengths)
    )
    highest = highest.reshape(requests, step_count, head_count)
    weight_sum = weight_sum.reshape(requests, step_count, head_count)
    weighted = weighted.reshape(requests, step_count, head_count, latent_width)
    projected_first = False
    global_peak = lax.pmax(highest, ("seq", "head"))
    rescale = jnp.exp(highest - global_peak)
    summed_weight, summed_latent = lax.psum(
        (weight_sum * rescale, weighted * rescale[..., None]), ("seq", "head")
    )
    peak_own = own_heads(global_peak, heads_own)
    sum_own = own_heads(summed_weight, heads_own)
    mixed_own = own_heads(summed_latent, heads_own)
    new_scores = (
        jnp.einsum("sbhc,tbc->bsht", own_queries, new_keys, preferred_element_type=jnp.float32)
        * softmax_scale
    )
    step_index = jnp.arange(step_count, dtype=jnp.int32)
    causal = (step_index[None, :] <= step_index[:, None])[None, :, None, :]
    new_scores = jnp.where(causal, new_scores, masked_score)
    overall = jnp.maximum(peak_own, jnp.max(new_scores, axis=3))
    carried = jnp.exp(peak_own - overall)
    new_weights = jnp.where(causal, jnp.exp(new_scores - overall[..., None]), 0.0)
    denominator = sum_own * carried + jnp.sum(new_weights, axis=3)
    new_term = jnp.einsum(
        "bsht,tbc->bshc",
        new_weights.astype(jnp.bfloat16),
        new_keys[..., :latent_width],
        preferred_element_type=jnp.float32,
    )
    latent_out = (mixed_own * carried[..., None] + new_term) / denominator[..., None]
    result = project_values(latent_out, values_float)
    return jnp.swapaxes(result, 0, 1).astype(jnp.bfloat16)


def solution(mesh):
    in_specs = (
        P(None, None, "head", None),
        P("head", None, None),
        P("head", None, None),
        P(None, ("seq", "head"), None),
        P(),
        P(),
        P(),
    )
    out_specs = P(None, None, "head", None)
    return jax.shard_map(
        on_device, mesh=mesh, in_specs=in_specs, out_specs=out_specs, check_vma=False
    )
```

profile of v0, /device:TPU:0, one launch (start us, length us, event | category | flops | bytes accessed | tf_op | source)
XLA Modules:
  0.0 249.7 jit_solution(15587933454435357556)
XLA Ops:
  6.5 0.0 copy-start
  6.5 0.0 all-gather.2.cloned.1.call-start
  6.6 1.0 slice.28
  7.5 0.8 slice.27
  8.4 0.7 slice.32
  9.1 0.7 add_convert_fusion.2
  9.8 0.1 subtract_convert_fusion.1
  10.0 0.0 copy-done
  10.0 0.4 fusion.25
  10.4 0.0 copy-start.3
  10.4 0.1 subtract_convert_fusion
  10.6 0.9 pad_maximum_fusion
  11.5 0.0 all-gather.2.cloned.1.call-update
  11.5 0.0 all-reduce.2.cloned.1.call-start
  11.6 21.0 %all-gather.2.cloned.1.call-done = bf16[4,4,64,576]{3,1,0,2:T(4,128)(2,1)} async-done(((bf16[4,4,16,576]{3,1,0,2:T(4,128)(2,1)}), bf16[4,4,64,576]{3,1,0,2:T(4,128)(2,1)}) %all-gather.2.cloned.1.call-update) | async-done | bytes 1179664 | tf_op jit(solution)/shard_map/all_gather | solution.py:58
  32.6 1.6 copy.25
  34.2 0.0 copy-done.3
  34.2 26.1 %while.15 = (s32[]{:T(128)}, f32[4,256]{1,0:T(4,128)S(1)}, f32[4,256]{1,0:T(4,128)S(1)}, f32[4,256,512]{2,1,0:T(8,128)}, s32[4]{0:T(128)S(1)}, /*index=5*/bf16[4...) while((s32[]{:T(128)}, f32[4,256]{1,0:T(4,128)S(1)}, ...), condition=%wide.region_3.4_spmd.clone, body=%wide.region_0.3_spmd.clone.sunk | while | flops 1145572864 | bytes 16892552 | solution.py:82
  34.2 0.7 dynamic_slice.42
  34.9 0.7 add_compare_fusion.2
  35.6 1.8 dynamic-slice_bitcast_fusion.2
  37.5 1.1 fusion.74
  38.6 1.6 fusion.76
  40.1 0.5 fusion.75
  40.7 0.7 dynamic_slice.42
  41.4 0.7 add_compare_fusion.2
  42.1 1.8 dynamic-slice_bitcast_fusion.2
  44.0 1.1 fusion.74
  45.1 1.6 fusion.76
  46.7 0.5 fusion.75
  47.3 0.7 dynamic_slice.42
  47.9 0.7 add_compare_fusion.2
  48.6 1.8 dynamic-slice_bitcast_fusion.2
  50.5 1.1 fusion.74
  51.6 1.6 fusion.76
  53.2 0.5 fusion.75
  53.8 0.7 dynamic_slice.42
  54.5 0.7 add_compare_fusion.2
  55.2 1.8 dynamic-slice_bitcast_fusion.2
  57.0 1.1 fusion.74
  58.1 1.6 fusion.76
  59.7 0.5 fusion.75
  60.3 0.1 reshape.95
  60.4 39.3 %pmax.7 = f32[4,4,64]{2,1,0:T(4,128)S(1)} all-reduce(f32[4,4,64]{2,1,0:T(4,128)S(1)} %reshape.95), channel_id=1, replica_groups=mesh['seq'=8,'head'=4] {'seq','head'}, use_global_device_ids=true, to_apply=%region_4.5 | all-reduce | flops 1024 | bytes 8192 | tf_op jit(solution)/shard_map/pmax | solution.py:89
  99.7 0.1 reshape.96
  99.8 0.1 copy.26
  100.0 4.3 %copy_multiply_fusion = f32[4,4,64,512]{3,1,0,2:T(4,128)} fusion(f32[4,4,64,512]{3,2,1,0:T(8,128)} %bitcast.70, f32[4,4,64]{1,0,2:T(4,128)S(1)} %copy.26), kind=kLoop, calls=%fused_computation.21 | loop fusion | flops 524288 | bytes 4198400 | tf_op jit(solution)/shard_map/mul | solution.py:92
  104.3 0.0 copy-start.2
  104.3 0.0 copy-start.1
  104.3 0.0 all-reduce.2.cloned.1.call-update
  104.3 0.7 copy-done.2
  105.1 0.2 copy-done.1
  105.3 0.6 fusion.60
  105.9 41.4 %psum.15 = f32[4,4,64]{2,1,0:T(4,128)S(1)} all-reduce(f32[4,4,64]{2,1,0:T(4,128)S(1)} %bitcast.77), channel_id=1, replica_groups=mesh['seq'=8,'head'=4] {'seq','head'}, use_global_device_ids=true, to_apply=%region_7.8 | all-reduce | flops 1024 | bytes 8192 | tf_op jit(solution)/shard_map/psum | solution.py:91
  147.2 0.1 dynamic-slice_maximum_fusion
  147.3 0.1 fusion.42
  147.4 0.1 multiply_add_fusion
  147.5 0.1 copy.31
  147.6 0.1 copy.32
  147.7 0.3 fusion.48
  148.1 91.0 %all-reduce.2.cloned.1.call-done = f32[4,4,64,512]{3,1,0,2:T(4,128)} async-done(((f32[4,4,64,512]{3,1,0,2:T(4,128)}), f32[4,4,64,512]{3,1,0,2:T(4,128)}) %all-reduce.2.cloned.1.call-update) | async-done | bytes 2097168 | tf_op jit(solution)/shard_map/psum | solution.py:91
  239.1 3.1 %fusion.31 = bf16[4,4,16,128]{3,0,1,2:T(4,128)(2,1)S(1)} fusion(bf16[16,512,128]{2,1,0:T(8,128)(2,1)} %param.11, f32[4,4,16,512]{3,2,1,0:T(8,128)S(1)} %fusion.48, f32[4,4,64,512]{3,1,0,2:T(4,128)} %all-reduce.2.cloned.1.call-done, s32[]{:T(128)S(6)} %select_n.19, f32[4,4,16]{1,0,2:T(4,128)S(1)} %copy.32, f32[4,4,16]{1,0,2:T(4,128)S(1)} %copy.31), kind=kOutput, calls=%fused_computation.25 | convolution fusion | flops 201752576 | bytes 3213316 | tf_op jit(solution)/shard_map/bshc,hcv->bshv/dot_general | solution.py:37
  242.2 0.6 copy.33
  (24 shorter events, 0.6 us)
Async XLA Ops:
  6.5 3.5 %copy-start = (bf16[16,128,512]{2,1,0:T(8,128)(2,1)S(1)}, bf16[16,128,512]{2,1,0:T(8,128)(2,1)}, u32[]{:S(2)}) copy-start(bf16[16,128,512]{2,1,0:T(8,128)(2,1)} %param.10) | copy-start | bytes 6291460
  6.5 26.1 %all-gather.2.cloned.1.call-start = ((), (), s32[]{:S(2)}) async-start(), calls=%async_computation | async-start | bytes 1638400 | tf_op jit(solution)/shard_map/all_gather | solution.py:58
  10.4 23.8 %copy-start.3 = (s32[4]{0:T(128)S(1)}, s32[4]{0:T(128)}, u32[]{:S(2)}) copy-start(s32[4]{0:T(128)} %param.14) | copy-start | bytes 52
  11.5 227.6 %all-reduce.2.cloned.1.call-start = ((), (), s32[]{:S(2)}) async-start(), calls=%async_computation.1 | async-start | bytes 4194304 | tf_op jit(solution)/shard_map/psum | solution.py:91
  104.3 0.7 copy-start.2
  104.3 1.0 copy-start.1
Sparse Core Ops, SparseCore 0:
  11.7 20.8 all-gather.1
  104.4 134.6 all-reduce.1
where the time goes:
time: 250 us
  waiting for transfers between devices  112 us (45%)
  blocking collectives  80.7 us (32%)
  local copies, waits for them, and re-layouts  16.7 us (7%)
  matrix products  15.3 us (6%)
  between operations  13.6 us (5%)
  other arithmetic  11.3 us (5%)
    psum x1, waiting for transfers between devices, on_device(): lax.psum((weight_sum * rescale, weighted * rescale[..., None]), ('seq', '...  91 us
    psum x1, blocking collectives, on_device(): lax.psum((weight_sum * rescale, weighted * rescale[..., None]), ('seq', '...  41.4 us
    pmax x1, blocking collectives, on_device(): global_peak = lax.pmax(highest, ('seq', 'head'))  39.3 us
    all_gather x1, waiting for transfers between devices, on_device(): all_queries = lax.all_gather(own_queries, 'head', axis=2, tiled=True)  21 us
    squeeze x4, local copies, waits for them, and re-layouts, on_device(): lax.map(local_part, (jnp.swapaxes(all_queries, 0, 1), latent_cache, conte...  7.31 us
    dot_general x4, matrix products, local_part(): jnp.dot(weights.astype(jnp.bfloat16), cache_keys[:, :latent_width], prefe...  6.35 us
  transfers between devices with their start and end apart: 2, of which 2 were waited for; matrix products, arithmetic and copies ran while one was open for 1% of the time, Pallas kernels for 0%

commit v1 on v0

v1 whole, which is shorter than its diff:
```python
import functools

import jax
import jax.numpy as jnp
from jax import lax
from jax.experimental import pallas as pl
from jax.experimental.pallas import tpu as pltpu
from jax.sharding import PartitionSpec as P

MESH = pl.DeviceIdType.MESH
rope_base = 50000.0
masked_score = -1e30
lowest_peak = -1e29
log2_e = 1.4426950408889634
owners = 8
tile = 128
chunk = 512


def iota(shape, axis):
    return lax.broadcasted_iota(jnp.int32, shape, axis)


def rope_table(positions, steps, rope_width):
    halfway = rope_width // 2
    counter = jnp.arange(halfway, dtype=jnp.float32)
    inverse = jnp.power(jnp.float32(rope_base), -2.0 * counter / rope_width)
    grid = positions[None, :] + jnp.arange(steps, dtype=jnp.int32)[:, None]
    angles = grid.reshape(-1).astype(jnp.float32)[:, None] * inverse
    cosine, sine = jnp.cos(angles), jnp.sin(angles)
    return jnp.concatenate([cosine, cosine, -sine, sine], axis=-1)


def pack(values, peak, total):
    def term(v):
        return v.astype(jnp.bfloat16).astype(jnp.float32)

    p0 = term(peak)
    p1 = term(peak - p0)
    p2 = peak - p0 - p1
    t0 = term(total)
    t1 = total - t0
    shape = peak.shape[:-1] + (tile,)
    lane = iota(shape, len(shape) - 1)
    stats = jnp.where(lane == 0, p0, jnp.where(lane == 1, p1, jnp.where(lane == 2, p2, jnp.where(lane == 3, t0, t1))))
    return values.astype(jnp.bfloat16), stats.astype(jnp.bfloat16)


def unpack(packed, width):
    values = packed[..., :width].astype(jnp.float32)
    stats = packed[..., width:].astype(jnp.float32)
    peak = stats[..., 0:1] + stats[..., 1:2] + stats[..., 2:3]
    total = stats[..., 3:4] + stats[..., 4:5]
    return values, peak, total


def merge(one, two):
    (va, pa, ta), (vb, pb, tb) = one, two
    peak = jnp.maximum(pa, pb)
    wa, wb = jnp.exp2(pa - peak), jnp.exp2(pb - peak)
    return va * wa + vb * wb, peak, ta * wa + tb * wb


def kernel(
    seq_size,
    lengths,
    q_ref,
    new_ref,
    table_ref,
    up_keys_hbm,
    up_values_hbm,
    cache_hbm,
    out_ref,
    up_keys,
    up_values,
    cache,
    queries,
    new_keys,
    scores,
    partial,
    a_in,
    b_out,
    kept,
    b_in,
    c_out,
    c_in,
    gathered,
    load_sem,
    key_sem,
    value_sem,
    q1_send,
    q1_recv,
    qy_send,
    qy_recv,
    qf_send,
    qf_recv,
    a_send,
    a_recv,
    b_send,
    b_recv,
    c_send,
    c_recv,
    g_send,
    g_recv,
):
    steps, requests, heads, query_width = q_ref.shape
    nope, width = up_keys.shape[1], up_keys.shape[2]
    rope = query_width - nope
    rows_cached = cache.shape[1]
    rows = steps * heads
    piece = rows // owners
    all_rows = 4 * rows
    seq = lax.axis_index("seq")
    head = lax.axis_index("head")
    low = lax.rem(head, 2)
    high = lax.div(head, 2)
    near = head + 1 - 2 * low
    across = lax.rem(head + 2, 4)
    slot = seq * 4 + head
    owned = lax.rem(seq, owners)

    def at_head(h):
        return (seq, h)

    barrier = pltpu.get_barrier_semaphore()
    for h in (near, across):
        pl.semaphore_signal(barrier, inc=1, device_id=at_head(h), device_id_type=MESH)
    for d in range(1, seq_size):
        pl.semaphore_signal(barrier, inc=1, device_id=(lax.rem(seq + d, seq_size), head), device_id_type=MESH)

    key_load = pltpu.make_async_copy(up_keys_hbm, up_keys, key_sem)
    key_load.start()
    value_load = pltpu.make_async_copy(up_values_hbm.at[pl.ds(owned * 2, 2)], up_values, value_sem)

    def load(b):
        return pltpu.make_async_copy(cache_hbm.at[b], cache.at[b], load_sem.at[b])

    for b in range(requests):
        load(b).start()
    value_load.start()

    swap = (iota((rope, rope), 0) == lax.rem(iota((rope, rope), 1) + rope // 2, rope)).astype(jnp.bfloat16)
    cosine = table_ref[:, :rope]
    sine = table_ref[:, rope:]
    flat = q_ref[...].reshape(steps * requests * heads, query_width)
    q_rope = flat[:, nope:]
    swapped = jnp.dot(q_rope, swap, preferred_element_type=jnp.float32)
    three = (steps * requests, heads, rope)
    rotated = (
        q_rope.astype(jnp.float32).reshape(three) * cosine[:, None, :] + swapped.reshape(three) * sine[:, None, :]
    )
    rotated = rotated.astype(jnp.bfloat16).reshape(steps * requests * heads, rope)
    count = steps * requests * heads
    row = iota((count, count), 0)
    wanted = (row & (steps - 1)) * (requests * heads) + lax.div(row, rows) * heads + lax.div(lax.rem(row, rows), steps)
    order = (iota((count, count), 1) == wanted).astype(jnp.bfloat16)
    q_nope = jnp.dot(order, flat[:, :nope], preferred_element_type=jnp.float32).astype(jnp.bfloat16)
    rotated = jnp.dot(order, rotated, preferred_element_type=jnp.float32).astype(jnp.bfloat16)

    new_flat = new_ref[...]
    new_rope = new_flat[:, width:]
    new_swapped = jnp.dot(new_rope, swap, preferred_element_type=jnp.float32)
    new_rotated = new_rope.astype(jnp.float32) * cosine + new_swapped * sine
    new_keys[...] = jnp.zeros_like(new_keys)
    new_keys[: steps * requests, :width] = new_flat[:, :width]
    new_keys[: steps * requests, width:] = new_rotated.astype(jnp.bfloat16)

    own_head = lax.div(lax.rem(iota((count, nope), 0), rows), steps)
    spread = jnp.concatenate(
        [jnp.where(own_head == h, q_nope.astype(jnp.float32), 0.0).astype(jnp.bfloat16) for h in range(heads)], axis=1
    )
    key_load.wait()
    latent = jnp.dot(spread, up_keys[...].reshape(heads * nope, width), preferred_element_type=jnp.float32)
    latent = latent.astype(jnp.bfloat16)
    for b in range(requests):
        queries[b, head, :, :width] = latent[b * rows : (b + 1) * rows]
        queries[b, head, :, width:] = rotated[b * rows : (b + 1) * rows]

    def remote(source, target, send, recv, device):
        return pltpu.make_async_remote_copy(
            src_ref=source, dst_ref=target, send_sem=send, recv_sem=recv, device_id=device, device_id_type=MESH
        )

    def q_near(b):
        block = queries.at[b, head]
        return remote(block, block, q1_send.at[b], q1_recv.at[b], at_head(near))

    def q_across(b):
        block = queries.at[b, head]
        return remote(block, block, qy_send.at[b], qy_recv.at[b], at_head(across))

    def q_forward(b):
        block = queries.at[b, across]
        return remote(block, block, qf_send.at[b], qf_recv.at[b], at_head(near))

    def a_copy(b, j):
        return remote(
            partial.at[b, 1 - low + 2 * j], a_in.at[b, j], a_send.at[b, j], a_recv.at[b, j], at_head(near)
        )

    def b_copy(b):
        return remote(b_out.at[b], b_in.at[b], b_send.at[b], b_recv.at[b], at_head(across))

    def c_copy(p, target, source):
        return remote(
            c_out.at[p, target], c_in.at[p, source], c_send.at[p, target], c_recv.at[p, source], (target, head)
        )

    def g_copy(d):
        target = lax.rem(seq + d, seq_size)
        return remote(
            gathered.at[owned], gathered.at[owned], g_send.at[target], g_recv.at[owned], (target, head)
        )

    pl.semaphore_wait(barrier, 2 + seq_size - 1)
    for b in range(requests):
        q_across(b).start()
        q_near(b).start()

    q_across(0).wait_recv()
    q_forward(0).start()

    factor = log2_e * float(query_width) ** (-0.5)

    def attend(b):
        q_near(b).wait_recv()
        q_forward(b).wait_recv()
        load(b).wait()
        q = queries[b].reshape(all_rows, width + rope)
        length = lengths[b]
        peaks = jnp.full((all_rows, tile), lowest_peak, jnp.float32)

        def tiles(x, op, start):
            for i in range(x.shape[1] // tile):
                start = op(start, x[:, i * tile : (i + 1) * tile])
            return start

        nt = (((1,), (1,)), ((), ()))
        for c in range(rows_cached // chunk):
            s = lax.dot_general(
                q, cache[b, c * chunk : (c + 1) * chunk, :], nt, preferred_element_type=jnp.float32
            )
            number = slot * rows_cached + c * chunk + iota((1, chunk), 1)
            x = s * factor + jnp.where(number < length, 0.0, masked_score)
            scores[:, c * chunk : (c + 1) * chunk] = x
            peaks = tiles(x, jnp.maximum, peaks)
        s = lax.dot_general(q, new_keys[...], nt, preferred_element_type=jnp.float32)
        column = iota((all_rows, tile), 1)
        step = iota((all_rows, tile), 0) & (steps - 1)
        fresh = (
            (lax.rem(column, requests) == b)
            & (lax.div(column, requests) <= step)
            & (column < steps * requests)
            & (slot == 0)
        )
        x_new = s * factor + jnp.where(fresh, 0.0, masked_score)
        peak = jnp.max(jnp.maximum(peaks, x_new), axis=1, keepdims=True)

        @pl.when(b < requests - 1)
        def _():
            q_across(b + 1).wait_recv()
            q_forward(b + 1).start()

        weights = jnp.exp2(x_new - peak)
        totals = weights
        total_out = jnp.dot(weights.astype(jnp.bfloat16), new_keys[:, :width], preferred_element_type=jnp.float32)
        for c in range(rows_cached // chunk):
            weights = jnp.exp2(scores[:, c * chunk : (c + 1) * chunk] - peak)
            totals = tiles(weights, jnp.add, totals)
            total_out += jnp.dot(
                weights.astype(jnp.bfloat16),
                cache[b, c * chunk : (c + 1) * chunk, :width],
                preferred_element_type=jnp.float32,
            )
        total = jnp.sum(totals, axis=1, keepdims=True)
        values, stats = pack(total_out, peak, total)
        partial[b, :, :, :width] = values.reshape(4, rows, width)
        partial[b, :, :, width:] = stats.reshape(4, rows, tile)
        for j in range(2):
            a_copy(b, j).start()

    def merge_near(b):
        for j in range(2):
            a_copy(b, j).wait_recv()
        other = 1 - high
        merged = merge(
            unpack(partial[b, low + 2 * other], width),
            unpack(a_in[b, other], width),
        )
        values, stats = pack(*merged)
        b_out[b, :, :width] = values
        b_out[b, :, width:] = stats
        b_copy(b).start()
        values, peak, total = merge(
            unpack(partial[b, head], width),
            unpack(a_in[b, high], width),
        )
        kept[b, :, :width] = values
        kept[b, :, width:] = jnp.where(iota((rows, tile), 1) == 0, peak, total)

    def merge_across(b):
        b_copy(b).wait_recv()
        mine = (kept[b, :, :width], kept[b, :, width : width + 1], kept[b, :, width + 1 : width + 2])
        values, peak, total = merge(mine, unpack(b_in[b], width))
        kept[b, :, :width] = values
        kept[b, :, width:] = jnp.where(iota((rows, tile), 1) == 0, peak, total)

    def send_pair(p):
        both = jnp.concatenate(
            [kept[2 * p + i].reshape(owners, piece, width + tile) for i in range(2)], axis=1
        )
        values, stats = pack(both[..., :width], both[..., width : width + 1], both[..., width + 1 : width + 2])
        c_out[p, :, :, :width] = values
        c_out[p, :, :, width:] = stats
        for d in range(0 if seq_size > owners else 1, owners):
            target = lax.rem(seq + d, owners)
            if d == 0:
                @pl.when(seq >= owners)
                def _():
                    c_copy(p, target, seq).start()
            else:
                c_copy(p, target, seq).start()

    def finish_pair(p):
        c_in[p, owned] = c_out[p, owned]
        for d in range(1, seq_size):
            c_copy(p, owned, lax.rem(seq + d, seq_size)).wait_recv()
        values, peaks, totals = unpack(c_in[p], width)
        peak = jnp.max(peaks, axis=0, keepdims=True)
        scale = jnp.exp2(peaks - peak)
        mixed = jnp.sum(values * scale, axis=0) / jnp.sum(totals * scale, axis=0)
        both = 2 * piece
        second = lax.rem(iota((both, width), 0), piece) >= steps
        wide = jnp.concatenate([jnp.where(second, 0.0, mixed), jnp.where(second, mixed, 0.0)], axis=1)
        w0 = wide.astype(jnp.bfloat16)
        rest = wide - w0.astype(jnp.float32)
        w1 = rest.astype(jnp.bfloat16)
        w2 = (rest - w1.astype(jnp.float32)).astype(jnp.bfloat16)
        matrix = up_values[...].reshape(2 * width, up_values.shape[2])
        result = sum(jnp.dot(w, matrix, preferred_element_type=jnp.float32) for w in (w2, w1, w0))
        gathered[owned, p * both : (p + 1) * both, :] = result.astype(jnp.bfloat16)

    def body(b, carry):
        attend(b)

        @pl.when(b >= 1)
        def _():
            merge_near(b - 1)

        @pl.when(b >= 2)
        def _():
            merge_across(b - 2)

        @pl.when(b == requests - 1)
        def _():
            send_pair(0)

        return carry

    lax.fori_loop(0, requests, body, 0)
    merge_near(requests - 1)
    merge_across(requests - 2)
    value_load.wait()

    def when_owner(fn):
        if seq_size > owners:
            pl.when(seq < owners)(fn)
        else:
            fn()

    when_owner(lambda: finish_pair(0))
    merge_across(requests - 1)
    send_pair(1)

    def last():
        finish_pair(1)
        for d in range(1, seq_size):
            g_copy(d).start()

    when_owner(last)

    def from_owner(j):
        block = gathered.at[j]
        return remote(block, block, g_send.at[j], g_recv.at[j], (seq, near))

    for d in range(0 if seq_size > owners else 1, owners):
        source = lax.rem(seq + d, owners)
        if d == 0:
            @pl.when(seq >= owners)
            def _():
                from_owner(source).wait_recv()
        else:
            from_owner(source).wait_recv()

    per = rows * requests // owners
    row = iota((count, count), 0)
    s_of = lax.div(row, requests * heads)
    b_of = lax.rem(lax.div(row, heads), requests)
    h_of = lax.rem(row, heads)
    source = (
        lax.div(h_of, 2) * per + lax.div(b_of, 2) * (2 * piece) + (b_of & 1) * piece + (h_of & 1) * steps + s_of
    )
    back = (iota((count, count), 1) == source).astype(jnp.bfloat16)
    result = jnp.dot(back, gathered[...].reshape(count, -1), preferred_element_type=jnp.float32)
    out_ref[...] = result.astype(jnp.bfloat16).reshape(out_ref.shape)

    for b in range(requests):
        q_near(b).wait_send()
        q_across(b).wait_send()
        q_forward(b).wait_send()
        for j in range(2):
            a_copy(b, j).wait_send()
        b_copy(b).wait_send()
    for p in range(2):
        for d in range(0 if seq_size > owners else 1, owners):
            target = lax.rem(seq + d, owners)
            if d == 0:
                @pl.when(seq >= owners)
                def _():
                    c_copy(p, target, seq).wait_send()
            else:
                c_copy(p, target, seq).wait_send()

    def sent():
        for d in range(1, seq_size):
            g_copy(d).wait_send()

    when_owner(sent)


def on_device(seq_size, query_heads, up_keys, up_values, latent_cache, new_latent, context_lengths, positions):
    steps, requests, heads, query_width = query_heads.shape
    nope, width = up_keys.shape[1:]
    value_width = up_values.shape[2]
    key_width = latent_cache.shape[2]
    cached = latent_cache.shape[1]
    rows = steps * heads
    table = rope_table(positions, steps, query_width - nope)
    bf16, f32 = jnp.bfloat16, jnp.float32
    packed = width + tile
    dma = pltpu.SemaphoreType.DMA
    vmem = pl.BlockSpec(memory_space=pltpu.VMEM)
    anywhere = pl.BlockSpec(memory_space=pl.ANY)
    return pl.pallas_call(
        functools.partial(kernel, seq_size),
        out_shape=jax.ShapeDtypeStruct((steps, requests, heads, value_width), bf16),
        in_specs=[pl.BlockSpec(memory_space=pltpu.SMEM), vmem, vmem, vmem, anywhere, anywhere, anywhere],
        out_specs=vmem,
        scratch_shapes=[
            pltpu.VMEM((heads, nope, width), bf16),
            pltpu.VMEM((2, width, value_width), bf16),
            pltpu.VMEM((requests, cached, key_width), bf16),
            pltpu.VMEM((requests, 4, rows, key_width), bf16),
            pltpu.VMEM((tile, key_width), bf16),
            pltpu.VMEM((4 * rows, cached), f32),
            pltpu.VMEM((requests, 4, rows, packed), bf16),
            pltpu.VMEM((requests, 2, rows, packed), bf16),
            pltpu.VMEM((requests, rows, packed), bf16),
            pltpu.VMEM((requests, rows, packed), f32),
            pltpu.VMEM((requests, rows, packed), bf16),
            pltpu.VMEM((2, owners, 2 * rows // owners, packed), bf16),
            pltpu.VMEM((2, seq_size, 2 * rows // owners, packed), bf16),
            pltpu.VMEM((owners, requests * rows // owners, value_width), bf16),
            dma((requests,)),
            dma,
            dma,
        ]
        + [dma((requests,))] * 6
        + [dma((requests, 2))] * 2
        + [dma((requests,))] * 2
        + [dma((2, owners)), dma((2, seq_size)), dma((seq_size,)), dma((owners,))],
        compiler_params=pltpu.CompilerParams(
            collective_id=0, has_side_effects=True, vmem_limit_bytes=56 * 1024 * 1024
        ),
        cost_estimate=pl.CostEstimate(
            flops=2 * requests * 4 * rows * cached * (key_width + width),
            bytes_accessed=2 * requests * cached * key_width,
            transcendentals=requests * 4 * rows * cached,
        ),
    )(
        context_lengths,
        query_heads,
        new_latent.reshape(steps * requests, key_width),
        table,
        up_keys,
        up_values,
        latent_cache,
    )


def solution(mesh):
    in_specs = (
        P(None, None, "head", None),
        P("head", None, None),
        P("head", None, None),
        P(None, ("seq", "head"), None),
        P(),
        P(),
        P(),
    )
    out_specs = P(None, None, "head", None)
    return jax.shard_map(
        functools.partial(on_device, mesh.shape["seq"]),
        mesh=mesh,
        in_specs=in_specs,
        out_specs=out_specs,
        check_vma=False,
    )
```

time: 250 us -> 62.4 us (0.25)
  waiting for transfers between devices: 112 us -> 0 us
  blocking collectives: 80.7 us -> 0 us
  Pallas kernels: 0 us -> 43.3 us
  matrix products: 15.3 us -> 0 us
  between operations: 13.6 us -> 0.02 us
  other arithmetic: 11.3 us -> 1.47 us
    psum x1 -> x0, waiting for transfers between devices: 91 us -> none  [on_device(): lax.psum((weight_sum * rescale, weighted * rescale[..., None]), ('seq', '...]
    pallas_call x0 -> x1, Pallas kernels: none -> 43.3 us  [on_device(): pl.pallas_call(functools.partial(kernel, seq_size), out_shape=jax.ShapeDt...]
    psum x1 -> x0, blocking collectives: 41.4 us -> none  [on_device(): lax.psum((weight_sum * rescale, weighted * rescale[..., None]), ('seq', '...]
    pmax x1 -> x0, blocking collectives: 39.3 us -> none  [on_device(): global_peak = lax.pmax(highest, ('seq', 'head'))]
    all_gather x1 -> x0, waiting for transfers between devices: 21 us -> none  [on_device(): all_queries = lax.all_gather(own_queries, 'head', axis=2, tiled=True)]
    dot_general x12 -> x0, matrix products: 15.3 us -> none  [the longest x4 6.35 us: local_part(): jnp.dot(weights.astype(jnp.bfloat16), cache_keys[:, :latent_width], prefe...]
    unnamed x10 -> x2, local copies, waits for them, and re-layouts: 2.53 us -> 15.6 us
    squeeze x4 -> x0, local copies, waits for them, and re-layouts: 7.31 us -> none  [on_device(): lax.map(local_part, (jnp.swapaxes(all_queries, 0, 1), latent_cache, conte...]
  transfers between devices with their start and end apart: 2 -> 0, of which waited for: 2 -> 0; matrix products, arithmetic and copies ran while one was open for 1% -> 0% of each run, Pallas kernels for 0% -> 0%
where the time goes in v1:
time: 62.4 us; the launch traced here: 61.8 us
  Pallas kernels  43.3 us (69%)
  local copies, waits for them, and re-layouts  17.1 us (27%)
  other arithmetic  1.47 us (2%)
    pallas_call x1, Pallas kernels, on_device(): pl.pallas_call(functools.partial(kernel, seq_size), out_shape=jax.ShapeDt...  43.3 us
    unnamed x2, local copies, waits for them, and re-layouts  15.6 us
    reshape x1, local copies, waits for them, and re-layouts, on_device(): new_latent.reshape(steps * requests, key_width)  1.35 us

profile of v1, /device:TPU:0, one launch (start us, length us, event | category | flops | bytes accessed | tf_op | source)
XLA Modules:
  0.0 61.8 jit_solution(10385949828109301717)
XLA Ops:
  0.0 0.7 %add_convert_fusion = f32[4,4]{1,0:T(4,128)S(1)} fusion(s32[4]{0:T(128)} %param.13), kind=kLoop, calls=%fused_computation.4 | loop fusion | flops 32 | bytes 80 | tf_op jit(solution)/shard_map/convert_element_type | solution.py:29
  0.7 0.1 convert_element_type.11
  0.8 1.4 %reshape.24.new_ref = bf16[16,576]{1,0:T(8,128)(2,1)} reshape(bf16[4,4,576]{2,1,0:T(4,128)(2,1)} %param.11) | data formatting | bytes 36864 | tf_op jit(solution)/shard_map/reshape | solution.py:483
  2.1 0.1 multiply_cosine_fusion
  2.2 0.7 %pad_maximum_fusion.table_ref = f32[16,128]{1,0:T(8,128)} fusion(f32[16,32]{1,0:T(8,128)S(1)} %get-tuple-element.7, f32[16,32]{1,0:T(8,128)S(1)} %get-tuple-element.6, f32[16,32]{1,0:T(8,128)S(1)} %get-tuple-element.5), kind=kLoop, calls=%fused_computation.2 | loop fusion | flops 6144 | bytes 14336 | tf_op jit(solution)/shard_map/concatenate | solution.py:31
  2.9 14.1 %copy.8.cache_hbm = bf16[4,2048,576]{2,1,0:T(8,128)(2,1)} copy(bf16[4,2048,576]{1,2,0:T(8,128)(2,1)} %param.10) | data formatting | bytes 18874368 | tf_op args[3]
  17.0 43.3 %shard_map.73 = bf16[4,4,16,128]{3,2,1,0:T(8,128)(2,1)} custom-call(s32[4]{0:T(128)} %lengths.1, bf16[4,4,16,192]{3,2,1,0:T(8,128)(2,1)} %q_ref.1, bf16[16,576]{1,0:T(8,128)(2,1)} %reshape.24.new_ref, f32[16,128]{1,0:T(8,128)} %pad_maximum_fusion.table_ref, bf16[16,128,512]{2,1,0:T(8,128)(2,1)} %up_keys_hbm.1, bf16[16,512,128]{2,1,0:T(8,128)(2,1)} %up_values_hbm.1, ...), custom_call_target="tpu_custom_call" | custom-call | flops 4563402752 | bytes 9437184 | tf_op jit(solution)/shard_map/pallas_call | solution.py:444
  60.3 1.5 %copy.10 = bf16[4,4,16,128]{3,2,1,0:T(8,128)(2,1)} copy(bf16[4,4,16,128]{3,2,1,0:T(8,128)(2,1)} %shard_map.73) | data formatting | bytes 131072
  (1 shorter events, 0.0 us)

commit v2 on v1

--- a/solution.py
+++ b/solution.py
@@ -2,6 +2,7 @@
 
 import jax
 import jax.numpy as jnp
+import numpy as np
 from jax import lax
 from jax.experimental import pallas as pl
 from jax.experimental.pallas import tpu as pltpu
@@ -15,20 +16,25 @@
 owners = 8
 tile = 128
 chunk = 512
+turn_high = np.float32(6.28125)
+turn_middle = np.float32(254 / 128 / 1024)
+turn_low = np.float32(2 * np.pi - 6.28125 - 254 / 128 / 1024)
 
 
 def iota(shape, axis):
     return lax.broadcasted_iota(jnp.int32, shape, axis)
 
 
-def rope_table(positions, steps, rope_width):
+def frequencies(rope_width):
     halfway = rope_width // 2
-    counter = jnp.arange(halfway, dtype=jnp.float32)
-    inverse = jnp.power(jnp.float32(rope_base), -2.0 * counter / rope_width)
-    grid = positions[None, :] + jnp.arange(steps, dtype=jnp.int32)[:, None]
-    angles = grid.reshape(-1).astype(jnp.float32)[:, None] * inverse
-    cosine, sine = jnp.cos(angles), jnp.sin(angles)
-    return jnp.concatenate([cosine, cosine, -sine, sine], axis=-1)
+    inverse = np.power(rope_base, -2.0 * np.arange(halfway) / rope_width).astype(np.float32)
+    return np.concatenate([inverse, inverse])[None, :]
+
+
+def cos_sin(angles):
+    turns = jnp.floor(angles * np.float32(0.5 / np.pi) + 0.5)
+    rest = ((angles - turns * turn_high) - turns * turn_middle) - turns * turn_low
+    return jnp.cos(rest), jnp.sin(rest)
 
 
 def pack(values, peak, total):
@@ -64,9 +70,10 @@
 def kernel(
     seq_size,
     lengths,
+    positions,
     q_ref,
     new_ref,
-    table_ref,
+    frequency_ref,
     up_keys_hbm,
     up_values_hbm,
     cache_hbm,
@@ -106,7 +113,7 @@
     steps, requests, heads, query_width = q_ref.shape
     nope, width = up_keys.shape[1], up_keys.shape[2]
     rope = query_width - nope
-    rows_cached = cache.shape[1]
+    rows_cached = cache.shape[2]
     rows = steps * heads
     piece = rows // owners
     all_rows = 4 * rows
@@ -140,8 +147,12 @@
     value_load.start()
 
     swap = (iota((rope, rope), 0) == lax.rem(iota((rope, rope), 1) + rope // 2, rope)).astype(jnp.bfloat16)
-    cosine = table_ref[:, :rope]
-    sine = table_ref[:, rope:]
+    grid_row = iota((steps * requests, rope), 0)
+    grid = lax.div(grid_row, requests)
+    for b in range(requests):
+        grid = grid + jnp.where(lax.rem(grid_row, requests) == b, positions[b], 0)
+    cosine, sine = cos_sin(grid.astype(jnp.float32) * frequency_ref[...])
+    sine = jnp.where(iota((steps * requests, rope), 1) < rope // 2, -sine, sine)
     flat = q_ref[...].reshape(steps * requests * heads, query_width)
     q_rope = flat[:, nope:]
     swapped = jnp.dot(q_rope, swap, preferred_element_type=jnp.float32)
@@ -157,7 +168,7 @@
     q_nope = jnp.dot(order, flat[:, :nope], preferred_element_type=jnp.float32).astype(jnp.bfloat16)
     rotated = jnp.dot(order, rotated, preferred_element_type=jnp.float32).astype(jnp.bfloat16)
 
-    new_flat = new_ref[...]
+    new_flat = new_ref[...].astype(jnp.float32).reshape(steps * requests, width + rope).astype(jnp.bfloat16)
     new_rope = new_flat[:, width:]
     new_swapped = jnp.dot(new_rope, swap, preferred_element_type=jnp.float32)
     new_rotated = new_rope.astype(jnp.float32) * cosine + new_swapped * sine
@@ -237,9 +248,7 @@
 
         nt = (((1,), (1,)), ((), ()))
         for c in range(rows_cached // chunk):
-            s = lax.dot_general(
-                q, cache[b, c * chunk : (c + 1) * chunk, :], nt, preferred_element_type=jnp.float32
-            )
+            s = jnp.dot(q, cache[b, :, c * chunk : (c + 1) * chunk], preferred_element_type=jnp.float32)
             number = slot * rows_cached + c * chunk + iota((1, chunk), 1)
             x = s * factor + jnp.where(number < length, 0.0, masked_score)
             scores[:, c * chunk : (c + 1) * chunk] = x
@@ -267,9 +276,10 @@
         for c in range(rows_cached // chunk):
             weights = jnp.exp2(scores[:, c * chunk : (c + 1) * chunk] - peak)
             totals = tiles(weights, jnp.add, totals)
-            total_out += jnp.dot(
+            total_out += lax.dot_general(
                 weights.astype(jnp.bfloat16),
-                cache[b, c * chunk : (c + 1) * chunk, :width],
+                cache[b, :width, c * chunk : (c + 1) * chunk],
+                nt,
                 preferred_element_type=jnp.float32,
             )
         total = jnp.sum(totals, axis=1, keepdims=True)
@@ -435,21 +445,21 @@
     key_width = latent_cache.shape[2]
     cached = latent_cache.shape[1]
     rows = steps * heads
-    table = rope_table(positions, steps, query_width - nope)
     bf16, f32 = jnp.bfloat16, jnp.float32
     packed = width + tile
     dma = pltpu.SemaphoreType.DMA
+    smem = pl.BlockSpec(memory_space=pltpu.SMEM)
     vmem = pl.BlockSpec(memory_space=pltpu.VMEM)
     anywhere = pl.BlockSpec(memory_space=pl.ANY)
     return pl.pallas_call(
         functools.partial(kernel, seq_size),
         out_shape=jax.ShapeDtypeStruct((steps, requests, heads, value_width), bf16),
-        in_specs=[pl.BlockSpec(memory_space=pltpu.SMEM), vmem, vmem, vmem, anywhere, anywhere, anywhere],
+        in_specs=[smem, smem, vmem, vmem, vmem, anywhere, anywhere, anywhere],
         out_specs=vmem,
         scratch_shapes=[
             pltpu.VMEM((heads, nope, width), bf16),
             pltpu.VMEM((2, width, value_width), bf16),
-            pltpu.VMEM((requests, cached, key_width), bf16),
+            pltpu.VMEM((requests, key_width, cached), bf16),
             pltpu.VMEM((requests, 4, rows, key_width), bf16),
             pltpu.VMEM((tile, key_width), bf16),
             pltpu.VMEM((4 * rows, cached), f32),
@@ -479,12 +489,13 @@
         ),
     )(
         context_lengths,
+        positions,
         query_heads,
-        new_latent.reshape(steps * requests, key_width),
-        table,
+        new_latent,
+        jnp.asarray(frequencies(query_width - nope)),
         up_keys,
         up_values,
-        latent_cache,
+        jnp.swapaxes(latent_cache, 1, 2),
     )
 
 

time: 62.4 us -> 44.9 us (0.72)
  local copies, waits for them, and re-layouts: 17.1 us -> 1.47 us
  other arithmetic: 1.47 us -> 0 us
    unnamed x2 -> x1, local copies, waits for them, and re-layouts: 15.6 us -> 1.47 us
    reshape x1 -> x0, local copies, waits for them, and re-layouts: 1.35 us -> none  [on_device(): new_latent.reshape(steps * requests, key_width)]
    concatenate x1 -> x0, other arithmetic: 0.67 us -> none  [rope_table(): return jnp.concatenate([cosine, cosine, -sine, sine], axis=-1)]
    convert_element_type x1 -> x0, other arithmetic: 0.66 us -> none  [rope_table(): angles = grid.reshape(-1).astype(jnp.float32)[:, None] * inverse]
where the time goes in v2:
time: 44.9 us; the launch traced here: 44.7 us
  Pallas kernels  43.2 us (96%)
  local copies, waits for them, and re-layouts  1.47 us (3%)
    pallas_call x1, Pallas kernels, on_device(): pl.pallas_call(functools.partial(kernel, seq_size), out_shape=jax.ShapeDt...  43.2 us
    unnamed x1, local copies, waits for them, and re-layouts  1.47 us

profile of v2, /device:TPU:0, one launch (start us, length us, event | category | flops | bytes accessed | tf_op | source)
XLA Modules:
  0.0 44.7 jit_solution(6966339230833652376)
XLA Ops:
  0.0 43.2 %shard_map.82 = bf16[4,4,16,128]{3,2,1,0:T(8,128)(2,1)} custom-call(s32[4]{0:T(128)} %lengths.1, s32[4]{0:T(128)} %positions.1, bf16[4,4,16,192]{3,2,1,0:T(8,128)(2,1)} %q_ref.1, bf16[4,4,576]{2,1,0:T(4,128)(2,1)} %new_ref.1, f32[1,64]{1,0:T(1,128)} %constant.2.clone.frequency_ref, bf16[16,128,512]{2,1,0:T(8,128)(2,1)} %up_keys_hbm.1, ...), custom_call_target="tpu_custom_call" | custom-call | flops 4563402752 | bytes 9437184 | tf_op jit(solution)/shard_map/pallas_call | solution.py:454
  43.2 1.5 %copy.10 = bf16[4,4,16,128]{3,2,1,0:T(8,128)(2,1)} copy(bf16[4,4,16,128]{3,2,1,0:T(8,128)(2,1)} %shard_map.82) | data formatting | bytes 131072

commit v3 on v2

--- a/solution.py
+++ b/solution.py
@@ -84,6 +84,7 @@
     queries,
     new_keys,
     scores,
+    weights,
     partial,
     a_in,
     b_out,
@@ -91,6 +92,7 @@
     b_in,
     c_out,
     c_in,
+    mixed_latent,
     gathered,
     load_sem,
     key_sem,
@@ -116,6 +118,7 @@
     rows_cached = cache.shape[2]
     rows = steps * heads
     piece = rows // owners
+    half = width // 2
     all_rows = 4 * rows
     seq = lax.axis_index("seq")
     head = lax.axis_index("head")
@@ -140,11 +143,7 @@
     value_load = pltpu.make_async_copy(up_values_hbm.at[pl.ds(owned * 2, 2)], up_values, value_sem)
 
     def load(b):
-        return pltpu.make_async_copy(cache_hbm.at[b], cache.at[b], load_sem.at[b])
-
-    for b in range(requests):
-        load(b).start()
-    value_load.start()
+        return pltpu.make_async_copy(cache_hbm.at[b], cache.at[b, pl.ds(0, width + rope)], load_sem.at[b])
 
     swap = (iota((rope, rope), 0) == lax.rem(iota((rope, rope), 1) + rope // 2, rope)).astype(jnp.bfloat16)
     grid_row = iota((steps * requests, rope), 0)
@@ -161,6 +160,7 @@
         q_rope.astype(jnp.float32).reshape(three) * cosine[:, None, :] + swapped.reshape(three) * sine[:, None, :]
     )
     rotated = rotated.astype(jnp.bfloat16).reshape(steps * requests * heads, rope)
+    rotated = jnp.concatenate([rotated, jnp.zeros_like(rotated)], axis=1)
     count = steps * requests * heads
     row = iota((count, count), 0)
     wanted = (row & (steps - 1)) * (requests * heads) + lax.div(row, rows) * heads + lax.div(lax.rem(row, rows), steps)
@@ -174,18 +174,22 @@
     new_rotated = new_rope.astype(jnp.float32) * cosine + new_swapped * sine
     new_keys[...] = jnp.zeros_like(new_keys)
     new_keys[: steps * requests, :width] = new_flat[:, :width]
-    new_keys[: steps * requests, width:] = new_rotated.astype(jnp.bfloat16)
+    new_keys[: steps * requests, width : width + rope] = new_rotated.astype(jnp.bfloat16)
 
     own_head = lax.div(lax.rem(iota((count, nope), 0), rows), steps)
     spread = jnp.concatenate(
         [jnp.where(own_head == h, q_nope.astype(jnp.float32), 0.0).astype(jnp.bfloat16) for h in range(heads)], axis=1
     )
     key_load.wait()
+    for b in range(requests):
+        load(b).start()
+    value_load.start()
     latent = jnp.dot(spread, up_keys[...].reshape(heads * nope, width), preferred_element_type=jnp.float32)
     latent = latent.astype(jnp.bfloat16)
     for b in range(requests):
         queries[b, head, :, :width] = latent[b * rows : (b + 1) * rows]
-        queries[b, head, :, width:] = rotated[b * rows : (b + 1) * rows]
+        queries[b, head, :, width : width + tile] = rotated[b * rows : (b + 1) * rows]
+        cache[b, width + rope :, :] = jnp.zeros((tile - rope, rows_cached), jnp.bfloat16)
 
     def remote(source, target, send, recv, device):
         return pltpu.make_async_remote_copy(
@@ -228,31 +232,34 @@
         q_across(b).start()
         q_near(b).start()
 
-    q_across(0).wait_recv()
-    q_forward(0).start()
-
     factor = log2_e * float(query_width) ** (-0.5)
-
-    def attend(b):
+    nt = (((1,), (1,)), ((), ()))
+    spans = [slice(c * chunk, (c + 1) * chunk) for c in range(rows_cached // chunk)]
+
+    def tiles(x, op, start):
+        for i in range(x.shape[1] // tile):
+            start = op(start, x[:, i * tile : (i + 1) * tile])
+        return start
+
+    def forward(b):
+        q_across(b).wait_recv()
+        q_forward(b).start()
+
+    def ready(b):
         q_near(b).wait_recv()
         q_forward(b).wait_recv()
         load(b).wait()
-        q = queries[b].reshape(all_rows, width + rope)
-        length = lengths[b]
-        peaks = jnp.full((all_rows, tile), lowest_peak, jnp.float32)
-
-        def tiles(x, op, start):
-            for i in range(x.shape[1] // tile):
-                start = op(start, x[:, i * tile : (i + 1) * tile])
-            return start
-
-        nt = (((1,), (1,)), ((), ()))
-        for c in range(rows_cached // chunk):
-            s = jnp.dot(q, cache[b, :, c * chunk : (c + 1) * chunk], preferred_element_type=jnp.float32)
-            number = slot * rows_cached + c * chunk + iota((1, chunk), 1)
-            x = s * factor + jnp.where(number < length, 0.0, masked_score)
-            scores[:, c * chunk : (c + 1) * chunk] = x
-            peaks = tiles(x, jnp.maximum, peaks)
+
+    def score(b, span, peaks):
+        q = queries[b].reshape(all_rows, width + tile)
+        s = jnp.dot(q, cache[b, :, span], preferred_element_type=jnp.float32)
+        number = slot * rows_cached + span.start + iota((1, chunk), 1)
+        x = s * factor + jnp.where(number < lengths[b], 0.0, masked_score)
+        scores[b % 2, :, span] = x
+        return tiles(x, jnp.maximum, peaks)
+
+    def score_new(b, peaks):
+        q = queries[b].reshape(all_rows, width + tile)
         s = lax.dot_general(q, new_keys[...], nt, preferred_element_type=jnp.float32)
         column = iota((all_rows, tile), 1)
         step = iota((all_rows, tile), 0) & (steps - 1)
@@ -262,32 +269,31 @@
             & (column < steps * requests)
             & (slot == 0)
         )
-        x_new = s * factor + jnp.where(fresh, 0.0, masked_score)
-        peak = jnp.max(jnp.maximum(peaks, x_new), axis=1, keepdims=True)
-
-        @pl.when(b < requests - 1)
-        def _():
-            q_across(b + 1).wait_recv()
-            q_forward(b + 1).start()
-
-        weights = jnp.exp2(x_new - peak)
-        totals = weights
-        total_out = jnp.dot(weights.astype(jnp.bfloat16), new_keys[:, :width], preferred_element_type=jnp.float32)
-        for c in range(rows_cached // chunk):
-            weights = jnp.exp2(scores[:, c * chunk : (c + 1) * chunk] - peak)
-            totals = tiles(weights, jnp.add, totals)
-            total_out += lax.dot_general(
-                weights.astype(jnp.bfloat16),
-                cache[b, :width, c * chunk : (c + 1) * chunk],
-                nt,
-                preferred_element_type=jnp.float32,
-            )
-        total = jnp.sum(totals, axis=1, keepdims=True)
-        values, stats = pack(total_out, peak, total)
+        x = s * factor + jnp.where(fresh, 0.0, masked_score)
+        return x, jnp.max(jnp.maximum(peaks, x), axis=1, keepdims=True)
+
+    lowest = jnp.full((all_rows, tile), lowest_peak, jnp.float32)
+
+    def attend(b, x_new, peak):
+        more = b + 1 < requests
+        peaks = lowest
+        fresh = jnp.exp2(x_new - peak)
+        totals = fresh
+        for span in spans:
+            if more:
+                peaks = score(b + 1, span, peaks)
+            w = jnp.exp2(scores[b % 2, :, span] - peak)
+            totals = tiles(w, jnp.add, totals)
+            weights[:, span] = w.astype(jnp.bfloat16)
+        following = score_new(b + 1, peaks) if more else None
+        mixed = jnp.dot(fresh.astype(jnp.bfloat16), new_keys[:, :width], preferred_element_type=jnp.float32)
+        mixed += lax.dot_general(weights[...], cache[b, :width, :], nt, preferred_element_type=jnp.float32)
+        values, stats = pack(mixed, peak, jnp.sum(totals, axis=1, keepdims=True))
         partial[b, :, :, :width] = values.reshape(4, rows, width)
         partial[b, :, :, width:] = stats.reshape(4, rows, tile)
         for j in range(2):
             a_copy(b, j).start()
+        return following
 
     def merge_near(b):
         for j in range(2):
@@ -311,36 +317,43 @@
     def merge_across(b):
         b_copy(b).wait_recv()
         mine = (kept[b, :, :width], kept[b, :, width : width + 1], kept[b, :, width + 1 : width + 2])
-        values, peak, total = merge(mine, unpack(b_in[b], width))
-        kept[b, :, :width] = values
-        kept[b, :, width:] = jnp.where(iota((rows, tile), 1) == 0, peak, total)
-
-    def send_pair(p):
-        both = jnp.concatenate(
-            [kept[2 * p + i].reshape(owners, piece, width + tile) for i in range(2)], axis=1
-        )
-        values, stats = pack(both[..., :width], both[..., width : width + 1], both[..., width + 1 : width + 2])
-        c_out[p, :, :, :width] = values
-        c_out[p, :, :, width:] = stats
+        values, stats = pack(*merge(mine, unpack(b_in[b], width)))
+        values = values.astype(jnp.float32).reshape(owners, piece, width)
+        stats = stats.astype(jnp.float32).reshape(owners, piece, tile)
+        c_out[b, :, :, :half] = jnp.concatenate([values[..., :half], values[..., half:]], axis=1).astype(jnp.bfloat16)
+        c_out[b, :, :, half:] = jnp.concatenate([stats, stats], axis=1).astype(jnp.bfloat16)
         for d in range(0 if seq_size > owners else 1, owners):
             target = lax.rem(seq + d, owners)
             if d == 0:
                 @pl.when(seq >= owners)
                 def _():
-                    c_copy(p, target, seq).start()
+                    c_copy(b, target, seq).start()
             else:
-                c_copy(p, target, seq).start()
-
-    def finish_pair(p):
-        c_in[p, owned] = c_out[p, owned]
-        for d in range(1, seq_size):
-            c_copy(p, owned, lax.rem(seq + d, seq_size)).wait_recv()
-        values, peaks, totals = unpack(c_in[p], width)
-        peak = jnp.max(peaks, axis=0, keepdims=True)
-        scale = jnp.exp2(peaks - peak)
-        mixed = jnp.sum(values * scale, axis=0) / jnp.sum(totals * scale, axis=0)
-        both = 2 * piece
-        second = lax.rem(iota((both, width), 0), piece) >= steps
+                c_copy(b, target, seq).start()
+
+    def when_owner(fn):
+        if seq_size > owners:
+            pl.when(seq < owners)(fn)
+        else:
+            fn()
+
+    def finish(b):
+        def combine():
+            c_in[b, owned] = c_out[b, owned]
+            for d in range(1, seq_size):
+                c_copy(b, owned, lax.rem(seq + d, seq_size)).wait_recv()
+            values, peaks, totals = unpack(c_in[b], half)
+            peak = jnp.max(peaks, axis=0, keepdims=True)
+            scale = jnp.exp2(peaks - peak)
+            mixed = jnp.sum(values * scale, axis=0) / jnp.sum(totals * scale, axis=0)
+            mixed_latent[b, :, :half] = mixed[:piece]
+            mixed_latent[b, :, half:] = mixed[piece:]
+
+        when_owner(combine)
+
+    def project():
+        mixed = mixed_latent[...].reshape(requests * piece, width)
+        second = lax.rem(iota(mixed.shape, 0), piece) >= steps
         wide = jnp.concatenate([jnp.where(second, 0.0, mixed), jnp.where(second, mixed, 0.0)], axis=1)
         w0 = wide.astype(jnp.bfloat16)
         rest = wide - w0.astype(jnp.float32)
@@ -348,42 +361,37 @@
         w2 = (rest - w1.astype(jnp.float32)).astype(jnp.bfloat16)
         matrix = up_values[...].reshape(2 * width, up_values.shape[2])
         result = sum(jnp.dot(w, matrix, preferred_element_type=jnp.float32) for w in (w2, w1, w0))
-        gathered[owned, p * both : (p + 1) * both, :] = result.astype(jnp.bfloat16)
-
-    def body(b, carry):
-        attend(b)
-
-        @pl.when(b >= 1)
-        def _():
+        gathered[owned] = result.astype(jnp.bfloat16)
+
+    forward(0)
+    forward(1)
+    ready(0)
+    peaks = lowest
+    for span in spans:
+        peaks = score(0, span, peaks)
+    following = score_new(0, peaks)
+    for b in range(requests):
+        if b + 2 < requests:
+            forward(b + 2)
+        if b + 1 < requests:
+            ready(b + 1)
+        following = attend(b, *following)
+        if b >= 1:
             merge_near(b - 1)
-
-        @pl.when(b >= 2)
-        def _():
+        if b >= 2:
             merge_across(b - 2)
-
-        @pl.when(b == requests - 1)
-        def _():
-            send_pair(0)
-
-        return carry
-
-    lax.fori_loop(0, requests, body, 0)
+        if b >= 3:
+            finish(b - 3)
     merge_near(requests - 1)
     merge_across(requests - 2)
+    finish(requests - 3)
     value_load.wait()
-
-    def when_owner(fn):
-        if seq_size > owners:
-            pl.when(seq < owners)(fn)
-        else:
-            fn()
-
-    when_owner(lambda: finish_pair(0))
     merge_across(requests - 1)
-    send_pair(1)
+    finish(requests - 2)
+    finish(requests - 1)
 
     def last():
-        finish_pair(1)
+        project()
         for d in range(1, seq_size):
             g_copy(d).start()
 
@@ -407,12 +415,10 @@
     s_of = lax.div(row, requests * heads)
     b_of = lax.rem(lax.div(row, heads), requests)
     h_of = lax.rem(row, heads)
-    source = (
-        lax.div(h_of, 2) * per + lax.div(b_of, 2) * (2 * piece) + (b_of & 1) * piece + (h_of & 1) * steps + s_of
-    )
+    source = lax.div(h_of, 2) * per + b_of * piece + (h_of & 1) * steps + s_of
     back = (iota((count, count), 1) == source).astype(jnp.bfloat16)
     result = jnp.dot(back, gathered[...].reshape(count, -1), preferred_element_type=jnp.float32)
-    out_ref[...] = result.astype(jnp.bfloat16).reshape(out_ref.shape)
+    out_ref[...] = result.reshape(out_ref.shape)
 
     for b in range(requests):
         q_near(b).wait_send()
@@ -421,7 +427,7 @@
         for j in range(2):
             a_copy(b, j).wait_send()
         b_copy(b).wait_send()
-    for p in range(2):
+    for p in range(requests):
         for d in range(0 if seq_size > owners else 1, owners):
             target = lax.rem(seq + d, owners)
             if d == 0:
@@ -451,25 +457,27 @@
     smem = pl.BlockSpec(memory_space=pltpu.SMEM)
     vmem = pl.BlockSpec(memory_space=pltpu.VMEM)
     anywhere = pl.BlockSpec(memory_space=pl.ANY)
-    return pl.pallas_call(
+    attended = pl.pallas_call(
         functools.partial(kernel, seq_size),
-        out_shape=jax.ShapeDtypeStruct((steps, requests, heads, value_width), bf16),
+        out_shape=jax.ShapeDtypeStruct((steps, requests, heads, value_width), f32),
         in_specs=[smem, smem, vmem, vmem, vmem, anywhere, anywhere, anywhere],
         out_specs=vmem,
         scratch_shapes=[
             pltpu.VMEM((heads, nope, width), bf16),
             pltpu.VMEM((2, width, value_width), bf16),
-            pltpu.VMEM((requests, key_width, cached), bf16),
-            pltpu.VMEM((requests, 4, rows, key_width), bf16),
-            pltpu.VMEM((tile, key_width), bf16),
-            pltpu.VMEM((4 * rows, cached), f32),
+            pltpu.VMEM((requests, packed, cached), bf16),
+            pltpu.VMEM((requests, 4, rows, packed), bf16),
+            pltpu.VMEM((tile, packed), bf16),
+            pltpu.VMEM((2, 4 * rows, cached), f32),
+            pltpu.VMEM((4 * rows, cached), bf16),
             pltpu.VMEM((requests, 4, rows, packed), bf16),
             pltpu.VMEM((requests, 2, rows, packed), bf16),
             pltpu.VMEM((requests, rows, packed), bf16),
             pltpu.VMEM((requests, rows, packed), f32),
             pltpu.VMEM((requests, rows, packed), bf16),
-            pltpu.VMEM((2, owners, 2 * rows // owners, packed), bf16),
-            pltpu.VMEM((2, seq_size, 2 * rows // owners, packed), bf16),
+            pltpu.VMEM((requests, owners, 2 * rows // owners, width // 2 + tile), bf16),
+            pltpu.VMEM((requests, seq_size, 2 * rows // owners, width // 2 + tile), bf16),
+            pltpu.VMEM((requests, rows // owners, width), f32),
             pltpu.VMEM((owners, requests * rows // owners, value_width), bf16),
             dma((requests,)),
             dma,
@@ -478,7 +486,7 @@
         + [dma((requests,))] * 6
         + [dma((requests, 2))] * 2
         + [dma((requests,))] * 2
-        + [dma((2, owners)), dma((2, seq_size)), dma((seq_size,)), dma((owners,))],
+        + [dma((requests, owners)), dma((requests, seq_size)), dma((seq_size,)), dma((owners,))],
         compiler_params=pltpu.CompilerParams(
             collective_id=0, has_side_effects=True, vmem_limit_bytes=56 * 1024 * 1024
         ),
@@ -497,6 +505,7 @@
         up_values,
         jnp.swapaxes(latent_cache, 1, 2),
     )
+    return attended.astype(bf16)
 
 
 def solution(mesh):

time: 44.9 us -> 44.6 us (level)
  other arithmetic: 0 us -> 1.54 us
  local copies, waits for them, and re-layouts: 1.47 us -> 0 us
    convert_element_type x0 -> x1, other arithmetic: none -> 1.54 us  [on_device(): return attended.astype(bf16)]
    unnamed x1 -> x0, local copies, waits for them, and re-layouts: 1.47 us -> none
where the time goes in v3:
time: 44.6 us; the launch traced here: 44.4 us
  Pallas kernels  42.8 us (96%)
  other arithmetic  1.54 us (3%)
    pallas_call x1, Pallas kernels, on_device(): pl.pallas_call(functools.partial(kernel, seq_size), out_shape=jax.ShapeDt...  42.8 us
    convert_element_type x1, other arithmetic, on_device(): return attended.astype(bf16)  1.54 us

profile of v3, /device:TPU:0, one launch (start us, length us, event | category | flops | bytes accessed | tf_op | source)
XLA Modules:
  0.0 44.4 jit_solution(3357526132453662165)
XLA Ops:
  0.0 42.8 %shard_map.82 = f32[4,4,16,128]{3,2,1,0:T(8,128)} custom-call(s32[4]{0:T(128)} %lengths.1, s32[4]{0:T(128)} %positions.1, bf16[4,4,16,192]{3,2,1,0:T(8,128)(2,1)} %q_ref.1, bf16[4,4,576]{2,1,0:T(4,128)(2,1)} %new_ref.1, f32[1,64]{1,0:T(1,128)} %constant.2.clone.frequency_ref, bf16[16,128,512]{2,1,0:T(8,128)(2,1)} %up_keys_hbm.1, ...), custom_call_target="tpu_custom_call" | custom-call | flops 4563402752 | bytes 9437184 | tf_op jit(solution)/shard_map/pallas_call | solution.py:460
  42.8 1.5 %convert_element_type.3 = bf16[4,4,16,128]{3,2,1,0:T(8,128)(2,1)} convert(f32[4,4,16,128]{3,2,1,0:T(8,128)} %shard_map.82) | non-fusion elementwise | flops 32768 | bytes 196608 | tf_op jit(solution)/shard_map/convert_element_type | solution.py:508
